TPU v7x, 32 devices: a whole 2x2x4 slice. The times are simulated.
32 devices in a mesh: groups: 2 (over y), blk: 16 (over z, x, core).
Axes of the slice: x: 2, y: 2, z: 4, core: 2. Of those that a mesh axis runs over, the one named last changes fastest.
Arguments:
- crack_energy: float32 [32768], P(('groups', 'blk')), parts along dimension 0, may hold values from 0.05 to 4
- weights: float32 [8, 32768], P(None, ('groups', 'blk')), parts along dimension 1, may hold values from 0 to 0.25
- elastic_stress: float32 [6, 32768], P(None, ('groups', 'blk')), parts along dimension 1, may hold values from -6 to 6
- owner_rank: int32 [32768, 1], P(('groups', 'blk')), parts along dimension 0, may hold values from 0 to 15; in each aligned block of 1024 rows (0 to 1023, 1024 to 2047, ...) at most 128 rows name the same one
- local_block: int32 [32768], P(('groups', 'blk')), parts along dimension 0, may hold values from 0 to 255
- base_cell: int32 [32768], P(('groups', 'blk')), parts along dimension 0, may hold values from 0 to 26
- prior_damage: float32 [256, 16, 128], P(('groups', 'blk')), parts along dimension 0, may hold values from 0 to 0.6
- toughness: float32 [256, 16, 128], P(('groups', 'blk')), parts along dimension 0, may hold values from 0.5 to 2
- active_block: int32 [8192], P(('groups', 'blk')), parts along dimension 0, may hold values 0 or 1
Outputs:
- damage: float32 [256, 16, 128], P(('groups', 'blk')), parts along dimension 0
- degraded_stress: float32 [6, 32768], P(None, ('groups', 'blk')), parts along dimension 1
There are 2 independent parts, one for each index of `groups`. A program takes and returns all parts, laid end to end along the dimension named above; each array names one. Nothing has to cross between parts.
Inputs may be any that keep to these rules, and one draw needn't show every extreme that they name: `owner_rank`: among the rows of one device, at most 128 particles name one owner, a bound that some block reaches.
All inputs are finite; a program needn't handle non-finite values. No bound on the sum of `active_block` on one device may be relied on, other than what follows from the above.
Results may differ from a plain program's by a relative error of at most 0.00002.
Values sent between devices are 32-bit elements; how exact they have to be, the bound alone decides.
A program may use at most 64 MiB of HBM per device.

v0:
```python
import jax
import jax.numpy as jnp
from jax import lax
from jax.sharding import PartitionSpec as P

BY = 4
BZ = 32
SWEEPS = 4


length_scale = 2.0
stiff_floor = 0.001


def extended_2(cells, sides, width):
    for axis, dim in sides:
        count = lax.axis_size(axis)
        ends = count - 1
        head = lax.slice_in_dim(cells, 0, width, axis=dim)
        tail = lax.slice_in_dim(cells, cells.shape[dim] - width, cells.shape[dim], axis=dim)
        cells = jnp.concatenate(
            [
                lax.ppermute(tail, axis, [(i, (i + 1) % count) for i in range(ends)]),
                cells,
                lax.ppermute(head, axis, [((i + 1) % count, i) for i in range(ends)]),
            ],
            axis=dim,
        )
    return cells


def corner_offsets():
    corner = jnp.arange(8, dtype=jnp.int32)
    return (corner // 4, corner // 2 % 2, corner % 2)


def cell_live(active_block, blocks_x):
    grid = active_block.reshape(blocks_x, BY, BZ).astype(jnp.float32)
    return jnp.repeat(jnp.repeat(jnp.repeat(grid, 4, 0), 4, 1), 4, 2)


def relax(extended, energy, toughness, live):
    padded = jnp.pad(extended, ((0, 0), (1, 1), (1, 1)))
    beside = padded[2:, 1:-1, 1:-1] + padded[:-2, 1:-1, 1:-1]
    beside = beside + padded[1:-1, 2:, 1:-1] + padded[1:-1, :-2, 1:-1]
    beside = beside + padded[1:-1, 1:-1, 2:] + padded[1:-1, 1:-1, :-2]
    couple = toughness * length_scale
    return (
        live
        * (2.0 * energy + couple * beside)
        / (toughness / length_scale + 2.0 * energy + 6.0 * couple)
    )


def decode(cell_code, size_y, size_z):
    valid = cell_code >= 0
    safe_code = jnp.maximum(cell_code, 0)
    block_id = safe_code // 27
    base_id = safe_code % 27
    off_x, off_y, off_z = corner_offsets()
    shape_tail = (1,) * cell_code.ndim
    cell_x = (4 * (block_id // (BY * BZ)) + base_id // 9)[None] + off_x.reshape((8,) + shape_tail)
    cell_y = (4 * (block_id // BZ % BY) + base_id // 3 % 3)[None] + off_y.reshape((8,) + shape_tail)
    cell_z = (4 * (block_id % BZ) + base_id % 3)[None] + off_z.reshape((8,) + shape_tail)
    local_index = ((cell_x * size_y + cell_y) * size_z + cell_z).astype(jnp.int32)
    return (local_index, valid)


def run_sweeps(prior_damage, energy, toughness, live):
    damage = prior_damage
    for sweep in range(SWEEPS):
        extended = extended_2(damage, (("blk", 0),), 1)
        damage = relax(extended, energy, toughness, live)
    return damage


def body(
    crack_energy,
    weights,
    elastic_stress,
    owner_rank,
    local_block,
    base_cell,
    prior_damage,
    toughness,
    active_block,
):
    devices = lax.axis_size("blk")
    count = crack_energy.shape[0]
    capacity = 2 * count // devices
    size_x, size_y, size_z = prior_damage.shape
    cells_dev = size_x * size_y * size_z
    target = owner_rank[:, 0]
    sort_order = jnp.argsort(target, stable=True)
    tallies = jax.ops.segment_sum(jnp.ones_like(target), target, num_segments=devices)
    starts = jnp.cumsum(tallies) - tallies
    ranked = jnp.arange(count, dtype=jnp.int32) - starts[target[sort_order]]
    position = jnp.zeros((count,), jnp.int32).at[sort_order].set(ranked)
    buffer_index = target * capacity + position
    cell_code = local_block * 27 + base_cell
    codes = jnp.full((devices * capacity,), -1, jnp.int32).at[buffer_index].set(cell_code)
    codes = codes.reshape(1, devices, capacity)
    live = cell_live(active_block, size_x // 4)
    payload = jnp.concatenate([crack_energy[None, :], weights], axis=0)
    packed = jnp.zeros((9, devices * capacity), jnp.float32).at[:, buffer_index].set(payload)
    packed = packed.reshape(9, devices, capacity)
    arrived, arrived_codes = (
        lax.all_to_all(packed, "blk", split_axis=1, concat_axis=1, tiled=True),
        lax.all_to_all(codes, "blk", split_axis=1, concat_axis=1, tiled=True),
    )
    local_index, valid = decode(arrived_codes[0], size_y, size_z)
    terms = jnp.where(valid[None], arrived[1:] * arrived[0:1], 0.0)
    energy = jnp.zeros((cells_dev,), jnp.float32).at[local_index.ravel()].add(terms.ravel())
    energy = energy.reshape(size_x, size_y, size_z)
    damage = run_sweeps(prior_damage, energy, toughness, live)
    sampled = jnp.sum(arrived[1:] * damage.ravel()[local_index], axis=0)
    returned = lax.all_to_all(sampled, "blk", split_axis=0, concat_axis=0, tiled=True)
    particle_damage = returned.reshape(-1)[buffer_index]
    factor = (1.0 - particle_damage) ** 2 + stiff_floor
    return (damage, factor[None, :] * elastic_stress)


def solution(mesh):
    return jax.shard_map(
        body,
        mesh=mesh,
        in_specs=(
            P(("groups", "blk")),
            P(None, ("groups", "blk")),
            P(None, ("groups", "blk")),
            P(("groups", "blk"), None),
            P(("groups", "blk")),
            P(("groups", "blk")),
            P(("groups", "blk"), None, None),
            P(("groups", "blk"), None, None),
            P(("groups", "blk")),
        ),
        out_specs=(P(("groups", "blk"), None, None), P(None, ("groups", "blk"))),
        check_vma=False,
    )
```

profile of v0, /device:TPU:0, one launch (start us, length us, event | category | flops | bytes accessed | tf_op | source)
XLA Modules:
  0.0 307.4 jit_solution(5652532644991378795)
XLA Ops:
  0.6 0.7 copy-done.1
  1.3 7.6 %scatter_custom_fusion = s32[16]{0:T(128)S(1)} fusion(s32[1024]{0:T(1024)S(1)} %bitcast.50, s32[1024]{0:T(1024)S(1)} %broadcast.424, s32[]{:T(128)} %constant.144.clone.1), kind=kCustom, calls=%fused_computation.160 | custom fusion | flops 1024 | bytes 68 | tf_op jit(solution)/shard_map/scatter-add | solution.py:95
  9.2 0.7 fusion.54
  9.9 4.4 %sort.17 = (s32[1024]{0:T(1024)}, s32[1024]{0:T(1024)S(1)}) sort(s32[1024]{0:T(1024)S(1)} %bitcast.51, s32[1024]{0:T(1024)S(1)} %iota.31), dimensions={0}, to_apply=%region_0.0 | sort | flops 10240 | bytes 16384 | tf_op jit(solution)/shard_map/jit(argsort)/sort | solution.py:94
  14.3 4.5 %gather_fusion = s32[1024]{0:T(1024)S(1)} fusion(s32[1024]{0:T(1024)S(1)} %bitcast.52, s32[1024]{0:T(1024)S(1)} %get-tuple-element.38), kind=kCustom, calls=%fused_computation | custom fusion | bytes 12288 | tf_op jit(solution)/shard_map/gather | solution.py:97
  18.8 4.4 %compare_select_fusion.3 = (s32[1024,1]{0,1:T(1,128)S(1)}, s32[1024,1]{0,1:T(1,128)S(1)}) fusion(s32[]{:T(128)} %bitcast.15, s32[]{:T(128)} %bitcast.16, s32[]{:T(128)} %bitcast.17, s32[]{:T(128)} %bitcast.18, s32[]{:T(128)} %bitcast.19, s32[]{:T(128)} %bitcast.21, s32[]{:T(128)} %bitcast.20, s32[1024,1]{0,1:T(1,128)S(1)} %bitcast.73), kind=kLoop, calls=%fused_computation.91 | loop fusion | flops 15360 | bytes 12316 | tf_op jit(solution)/shard_map/gather | solution.py:97
  23.3 5.6 %select_subtract_fusion = s32[1024]{0:T(1024)S(1)} fusion(pred[1024]{0:T(1024)(128)(4,1)S(1)} %get-tuple-element.22, pred[1024]{0:T(1024)(128)(4,1)S(1)} %get-tuple-element.21, pred[1024]{0:T(1024)(128)(4,1)S(1)} %get-tuple-element.20, pred[1024]{0:T(1024)(128)(4,1)S(1)} %get-tuple-element.19, pred[1024]{0:T(1024)(128)(4,1)S(1)} %get-tuple-element.18, ...), kind=kLoop, calls=%fused_computation.139 | loop fusion | flops 10240 | bytes 17444 | tf_op jit(solution)/shard_map/sub | solution.py:97
  29.0 4.3 %scatter_custom_fusion.1 = s32[1024]{0:T(1024)S(1)} fusion(s32[1024]{0:T(1024)S(1)} %get-tuple-element.39, s32[1024]{0:T(1024)S(1)} %select_subtract_fusion, s32[]{:T(128)} %constant.144.clone.1), kind=kCustom, calls=%fused_computation.148 | custom fusion | bytes 4100 | tf_op jit(solution)/shard_map/scatter | solution.py:98
  33.3 4.9 %scatter_custom_fusion.2 = s32[2048]{0:T(1024)} fusion(s32[1024]{0:T(1024)S(1)} %get-tuple-element.24, s32[1024]{0:T(1024)S(1)} %get-tuple-element.56, s32[]{:T(128)} %constant.142.clone.1), kind=kCustom, calls=%fused_computation.142 | custom fusion | bytes 8196 | tf_op jit(solution)/shard_map/scatter | solution.py:101
  38.2 7.4 %all-to-all-start = ((s32[1,16,128]{2,0,1:T(1,128)}), s32[1,16,128]{2,0,1:T(1,128)S(1)}, u32[]{:S(2)}, u32[]{:S(2)}) async-start(s32[1,16,128]{2,0,1:T(1,128)} %bitcast.23), calls=%async_computation | async-start | bytes 16384 | tf_op jit(solution)/shard_map/all_to_all | solution.py:109
  45.6 1.3 collective-permute-start
  46.9 3.0 collective-permute-start.1
  50.0 0.2 copy.202
  50.2 3.3 %scatter_custom_fusion.3 = f32[9,2048]{0,1:T(8,128)S(1)} fusion(s32[1024]{0:T(1024)S(1)} %get-tuple-element.24, f32[1024,9]{1,0:T(8,128)S(1)} %copy.202, f32[]{:T(128)} %constant.141.clone.1), kind=kCustom, calls=%fused_computation.8 | custom fusion | bytes 73732 | tf_op jit(solution)/shard_map/scatter | solution.py:105
  53.6 1.0 copy.203
  55.2 7.0 %all-to-all-start.1 = ((f32[9,16,128]{2,0,1:T(8,128)}), f32[9,16,128]{2,0,1:T(8,128)S(1)}, u32[]{:S(2)}, u32[]{:S(2)}) async-start(f32[9,16,128]{2,0,1:T(8,128)} %copy.203), calls=%async_computation.1 | async-start | bytes 262144 | tf_op jit(solution)/shard_map/all_to_all | solution.py:108
  62.5 7.7 %all-to-all-done.1 = f32[9,16,128]{2,0,1:T(8,128)S(1)} async-done(((f32[9,16,128]{2,0,1:T(8,128)}), f32[9,16,128]{2,0,1:T(8,128)S(1)}, u32[]{:S(2)}, u32[]{:S(2)}) %all-to-all-start.1) | async-done | bytes 73760 | tf_op jit(solution)/shard_map/all_to_all | solution.py:108
  70.2 86.0 %scatter_custom_fusion.4 = f32[16384]{0:T(1024)S(1)} fusion(s32[16384]{0:T(1024)S(1)} %bitcast.68, f32[16384]{0:T(1024)S(1)} %bitcast.69, f32[]{:T(128)} %constant.141.clone.1), kind=kCustom, calls=%fused_computation.78 | custom fusion | flops 16384 | bytes 65540 | tf_op jit(solution)/shard_map/scatter-add | solution.py:113
  156.2 0.8 copy-done.2
  157.2 1.3 collective-permute-start.2
  158.5 19.7 %collective-permute-start.3 = (f32[1,16,128]{2,1,0:T(8,128)S(1)}, f32[1,16,128]{2,1,0:T(8,128)S(1)}, u32[]{:S(2)}, u32[]{:S(2)}) collective-permute-start(f32[1,16,128]{2,1,0:T(8,128)S(1)} %get-tuple-element.31), channel_id=1, source_target_pairs={{0,1},{1,2},{2,3},{3,4},{4,5},{5,6},{6,7},{7,8},{8,9},{9,10},{10,1... | collective-permute-start | bytes 24584 | tf_op jit(solution)/shard_map/ppermute | solution.py:23
  178.2 0.8 collective-permute-done.3
  179.3 1.3 collective-permute-start.4
  180.6 4.2 %collective-permute-start.5 = (f32[1,16,128]{2,1,0:T(8,128)S(1)}, f32[1,16,128]{2,1,0:T(8,128)S(1)}, u32[]{:S(2)}, u32[]{:S(2)}) collective-permute-start(f32[1,16,128]{2,1,0:T(8,128)S(1)} %get-tuple-element.29), channel_id=1, source_target_pairs={{0,1},{1,2},{2,3},{3,4},{4,5},{5,6},{6,7},{7,8},{8,9},{9,10},{10,1... | collective-permute-start | bytes 24584 | tf_op jit(solution)/shard_map/ppermute | solution.py:23
  185.0 0.7 collective-permute-done.5
  186.0 1.3 collective-permute-start.6
  187.3 4.8 %collective-permute-start.7 = (f32[1,16,128]{2,1,0:T(8,128)S(1)}, f32[1,16,128]{2,1,0:T(8,128)S(1)}, u32[]{:S(2)}, u32[]{:S(2)}) collective-permute-start(f32[1,16,128]{2,1,0:T(8,128)S(1)} %get-tuple-element.27), channel_id=1, source_target_pairs={{0,1},{1,2},{2,3},{3,4},{4,5},{5,6},{6,7},{7,8},{8,9},{9,10},{10,1... | collective-permute-start | bytes 24584 | tf_op jit(solution)/shard_map/ppermute | solution.py:23
  192.1 0.8 collective-permute-done.7
  193.1 90.5 %gather_fusion.1 = f32[16384]{0:T(1024)S(1)} fusion(f32[16384]{0:T(1024)S(1)} %bitcast.49, s32[16384]{0:T(1024)S(1)} %broadcast_clamp_fusion), kind=kCustom, calls=%fused_computation.1 | custom fusion | bytes 196608 | tf_op jit(solution)/shard_map/gather | solution.py:116
  283.7 16.9 %all_to_all.19 = f32[16,1,128]{2,1,0:T(1,128)S(1)} all-to-all(f32[16,1,128]{2,1,0:T(1,128)S(1)} %bitcast.71), channel_id=1, replica_groups=mesh['groups'=2,'blk'=16] {'blk'}, dimensions={0} | all-to-all | bytes 16384 | tf_op jit(solution)/shard_map/all_to_all | solution.py:117
  300.6 6.1 %gather_fusion.2 = f32[1024]{0:T(1024)S(1)} fusion(f32[2048]{0:T(1024)S(1)} %bitcast.54, s32[1024]{0:T(1024)S(1)} %get-tuple-element.23), kind=kCustom, calls=%fused_computation.2 | custom fusion | bytes 12288 | tf_op jit(solution)/shard_map/gather | solution.py:118
  306.8 0.6 broadcast_multiply_fusion.1
  (68 shorter events, 2.4 us)
Async XLA Ops:
  0.6 0.7 copy-start.1
  18.8 14.5 %copy-start.7 = (s32[1024]{0:T(1024)S(1)}, s32[1024]{0:T(1024)}, u32[]{:S(2)}) copy-start(s32[1024]{0:T(1024)} %param.13) | copy-start | bytes 12292
  23.3 22.3 %copy-start.3 = (f32[8,16,128]{2,1,0:T(8,128)S(1)}, f32[8,16,128]{2,1,0:T(8,128)}, u32[]{:S(2)}) copy-start(f32[8,16,128]{2,1,0:T(8,128)} %param.15) | copy-start | bytes 196612
  29.0 4.3 %copy-start.6 = (s32[1024]{0:T(1024)S(1)}, s32[1024]{0:T(1024)}, u32[]{:S(2)}) copy-start(s32[1024]{0:T(1024)} %param.14) | copy-start | bytes 12292
  33.3 16.6 %copy-start.4 = (f32[8,1024]{1,0:T(8,128)S(1)}, f32[8,1024]{1,0:T(8,128)}, u32[]{:S(2)}) copy-start(f32[8,1024]{1,0:T(8,128)} %param.10) | copy-start | bytes 98308
  38.2 17.0 %all-to-all-start = ((s32[1,16,128]{2,0,1:T(1,128)}), s32[1,16,128]{2,0,1:T(1,128)S(1)}, u32[]{:S(2)}, u32[]{:S(2)}) async-start(s32[1,16,128]{2,0,1:T(1,128)} %bitcast.23), calls=%async_computation | async-start | bytes 16384 | tf_op jit(solution)/shard_map/all_to_all | solution.py:109
  45.6 4.4 %copy-start.8 = (f32[1024]{0:T(1024)S(1)}, f32[1024]{0:T(1024)}, u32[]{:S(2)}) copy-start(f32[1024]{0:T(1024)} %param.9) | copy-start | bytes 12292
  45.6 9.4 %collective-permute-start = (f32[1,16,128]{2,1,0:T(8,128)S(1)}, f32[1,16,128]{2,1,0:T(8,128)S(1)}, u32[]{:S(2)}, u32[]{:S(2)}) collective-permute-start(f32[1,16,128]{2,1,0:T(8,128)S(1)} %get-tuple-element.34), channel_id=1, source_target_pairs={{1,0},{2,1},{3,2},{4,3},{5,4},{6,5},{7,6},{8,7},{9,8},{10,9},{11,1... | collective-permute-start | bytes 24584 | tf_op jit(solution)/shard_map/ppermute | solution.py:25
  46.9 8.1 %collective-permute-start.1 = (f32[1,16,128]{2,1,0:T(8,128)S(1)}, f32[1,16,128]{2,1,0:T(8,128)S(1)}, u32[]{:S(2)}, u32[]{:S(2)}) collective-permute-start(f32[1,16,128]{2,1,0:T(8,128)S(1)} %get-tuple-element.33), channel_id=1, source_target_pairs={{0,1},{1,2},{2,3},{3,4},{4,5},{5,6},{6,7},{7,8},{8,9},{9,10},{10,1... | collective-permute-start | bytes 24584 | tf_op jit(solution)/shard_map/ppermute | solution.py:23
  53.6 1.0 copy-start.9
  55.2 15.0 %all-to-all-start.1 = ((f32[9,16,128]{2,0,1:T(8,128)}), f32[9,16,128]{2,0,1:T(8,128)S(1)}, u32[]{:S(2)}, u32[]{:S(2)}) async-start(f32[9,16,128]{2,0,1:T(8,128)} %copy.203), calls=%async_computation.1 | async-start | bytes 262144 | tf_op jit(solution)/shard_map/all_to_all | solution.py:108
  156.2 0.8 copy-start.2
  157.2 21.1 %collective-permute-start.2 = (f32[1,16,128]{2,1,0:T(8,128)S(1)}, f32[1,16,128]{2,1,0:T(8,128)S(1)}, u32[]{:S(2)}, u32[]{:S(2)}) collective-permute-start(f32[1,16,128]{2,1,0:T(8,128)S(1)} %get-tuple-element.32), channel_id=1, source_target_pairs={{1,0},{2,1},{3,2},{4,3},{5,4},{6,5},{7,6},{8,7},{9,8},{10,9},{11,1... | collective-permute-start | bytes 24584 | tf_op jit(solution)/shard_map/ppermute | solution.py:25
  158.5 20.6 %collective-permute-start.3 = (f32[1,16,128]{2,1,0:T(8,128)S(1)}, f32[1,16,128]{2,1,0:T(8,128)S(1)}, u32[]{:S(2)}, u32[]{:S(2)}) collective-permute-start(f32[1,16,128]{2,1,0:T(8,128)S(1)} %get-tuple-element.31), channel_id=1, source_target_pairs={{0,1},{1,2},{2,3},{3,4},{4,5},{5,6},{6,7},{7,8},{8,9},{9,10},{10,1... | collective-permute-start | bytes 24584 | tf_op jit(solution)/shard_map/ppermute | solution.py:23
  179.3 5.6 %collective-permute-start.4 = (f32[1,16,128]{2,1,0:T(8,128)S(1)}, f32[1,16,128]{2,1,0:T(8,128)S(1)}, u32[]{:S(2)}, u32[]{:S(2)}) collective-permute-start(f32[1,16,128]{2,1,0:T(8,128)S(1)} %get-tuple-element.30), channel_id=1, source_target_pairs={{1,0},{2,1},{3,2},{4,3},{5,4},{6,5},{7,6},{8,7},{9,8},{10,9},{11,1... | collective-permute-start | bytes 24584 | tf_op jit(solution)/shard_map/ppermute | solution.py:25
  180.6 5.0 %collective-permute-start.5 = (f32[1,16,128]{2,1,0:T(8,128)S(1)}, f32[1,16,128]{2,1,0:T(8,128)S(1)}, u32[]{:S(2)}, u32[]{:S(2)}) collective-permute-start(f32[1,16,128]{2,1,0:T(8,128)S(1)} %get-tuple-element.29), channel_id=1, source_target_pairs={{0,1},{1,2},{2,3},{3,4},{4,5},{5,6},{6,7},{7,8},{8,9},{9,10},{10,1... | collective-permute-start | bytes 24584 | tf_op jit(solution)/shard_map/ppermute | solution.py:23
  186.0 6.1 %collective-permute-start.6 = (f32[1,16,128]{2,1,0:T(8,128)S(1)}, f32[1,16,128]{2,1,0:T(8,128)S(1)}, u32[]{:S(2)}, u32[]{:S(2)}) collective-permute-start(f32[1,16,128]{2,1,0:T(8,128)S(1)} %get-tuple-element.28), channel_id=1, source_target_pairs={{1,0},{2,1},{3,2},{4,3},{5,4},{6,5},{7,6},{8,7},{9,8},{10,9},{11,1... | collective-permute-start | bytes 24584 | tf_op jit(solution)/shard_map/ppermute | solution.py:25
  187.3 5.6 %collective-permute-start.7 = (f32[1,16,128]{2,1,0:T(8,128)S(1)}, f32[1,16,128]{2,1,0:T(8,128)S(1)}, u32[]{:S(2)}, u32[]{:S(2)}) collective-permute-start(f32[1,16,128]{2,1,0:T(8,128)S(1)} %get-tuple-element.27), channel_id=1, source_target_pairs={{0,1},{1,2},{2,3},{3,4},{4,5},{5,6},{6,7},{7,8},{8,9},{9,10},{10,1... | collective-permute-start | bytes 24584 | tf_op jit(solution)/shard_map/ppermute | solution.py:23
  193.1 90.6 %copy-start = (f32[8,16,128]{2,1,0:T(8,128)}, f32[8,16,128]{2,1,0:T(8,128)S(1)}, u32[]{:S(2)}) copy-start(f32[8,16,128]{2,1,0:T(8,128)S(1)} %fusion.8) | copy-start | bytes 196612
  300.6 6.2 %copy-start.5 = (f32[6,1024]{1,0:T(8,128)S(1)}, f32[6,1024]{1,0:T(8,128)}, u32[]{:S(2)}) copy-start(f32[6,1024]{1,0:T(8,128)} %param.11) | copy-start | bytes 73732
where the time goes:
time: 308 us; the launch traced here: 307 us
  local copies, waits for them, and re-layouts  118 us (38%)
  other arithmetic  110 us (36%)
  starting transfers between devices  51.3 us (17%)
  blocking collectives  16.9 us (5%)
  waiting for transfers between devices  9.97 us (3%)
    gather x1, local copies, waits for them, and re-layouts, body(): sampled = jnp.sum(arrived[1:] * damage.ravel()[local_index], axis=0)  90.5 us
    scatter-add x1, other arithmetic, body(): jnp.zeros((cells_dev,), jnp.float32).at[local_index.ravel()]  86 us
    ppermute x4, starting transfers between devices, extended_2(): lax.ppermute(tail, axis, [(i, (i + 1) % count) for i in range(ends)])  31.8 us
    all_to_all x1, blocking collectives, body(): lax.all_to_all(sampled, 'blk', split_axis=0, concat_axis=0, tiled=True)  16.9 us
    all_to_all x1, waiting for transfers between devices, body(): lax.all_to_all(packed, 'blk', split_axis=1, concat_axis=1, tiled=True)  7.68 us
    scatter-add x1, other arithmetic, body(): jax.ops.segment_sum(jnp.ones_like(target), target, num_segments=devices)  7.61 us
    all_to_all x1, starting transfers between devices, body(): lax.all_to_all(codes, 'blk', split_axis=1, concat_axis=1, tiled=True)  7.36 us
    all_to_all x1, starting transfers between devices, body(): lax.all_to_all(packed, 'blk', split_axis=1, concat_axis=1, tiled=True)  7.01 us
  transfers between devices with their start and end apart: 10, of which 4 were waited for; matrix products, arithmetic and copies ran while one was open for 2% of the time, Pallas kernels for 0%

commit v1 on v0

v1 whole, which is shorter than its diff:
```python
import functools

import jax
import jax.numpy as jnp
from jax import lax
from jax.experimental import pallas as pl
from jax.experimental.pallas import tpu as pltpu
from jax.sharding import PartitionSpec as P

BY = 4
BZ = 32
SWEEPS = 4
LANES = 128
ROWS = 16

length_scale = 2.0
stiff_floor = 0.001

F32 = jnp.float32
BF16 = jnp.bfloat16


def iota(shape, axis):
    return lax.broadcasted_iota(jnp.int32, shape, axis)


def pieces(values):
    high = values.astype(BF16)
    rest = values - high.astype(F32)
    middle = rest.astype(BF16)
    low = (rest - middle.astype(F32)).astype(BF16)
    return high, middle, low


def dot_nt(left, right):
    return lax.dot_general(left, right, (((1,), (1,)), ((), ())), preferred_element_type=F32)


def dot_nn(left, right):
    return lax.dot_general(left, right, (((1,), (0,)), ((), ())), preferred_element_type=F32)


def loop(count, step, unrolled):
    if unrolled:
        for i in range(count):
            step(i)
    else:
        pl.loop(0, count)(step)


def kernel(
    n,
    size_x,
    size_y,
    energy_ref,
    weights_ref,
    stress_ref,
    owner_ref,
    block_ref,
    base_ref,
    prior_ref,
    tough_ref,
    active_ref,
    damage_ref,
    out_ref,
    send,
    arrived,
    mixed,
    zhot,
    total,
    energy_ext,
    tough_ext,
    prior_ext,
    back_send,
    back,
    send_sem,
    recv_sem,
    back_send_sem,
    back_recv_sem,
    side_send_sem,
    side_recv_sem,
):
    me = lax.axis_index("blk")
    cells = size_x * size_y
    count = owner_ref.shape[1]
    pad = SWEEPS * size_y
    inner = (SWEEPS - 1) * size_y
    unrolled = n <= 16

    def to(device):
        return {"blk": device}

    def side_copy(which, source, target, device):
        return pltpu.make_async_remote_copy(
            src_ref=source,
            dst_ref=target,
            send_sem=side_send_sem.at[which],
            recv_sem=side_recv_sem.at[which],
            device_id=to(device),
            device_id_type=pl.DeviceIdType.MESH,
        )

    def bucket_copy(device):
        return pltpu.make_async_remote_copy(
            src_ref=send.at[device],
            dst_ref=arrived.at[me],
            send_sem=send_sem.at[device],
            recv_sem=recv_sem.at[me],
            device_id=to(device),
            device_id_type=pl.DeviceIdType.MESH,
        )

    def bucket_arrival(device):
        return pltpu.make_async_remote_copy(
            src_ref=send.at[device],
            dst_ref=arrived.at[device],
            send_sem=send_sem.at[device],
            recv_sem=recv_sem.at[device],
            device_id=to(device),
            device_id_type=pl.DeviceIdType.MESH,
        )

    def back_copy(device):
        return pltpu.make_async_remote_copy(
            src_ref=back_send.at[device],
            dst_ref=back.at[me],
            send_sem=back_send_sem.at[device],
            recv_sem=back_recv_sem.at[me],
            device_id=to(device),
            device_id_type=pl.DeviceIdType.MESH,
        )

    def back_arrival(device):
        return pltpu.make_async_remote_copy(
            src_ref=back_send.at[device],
            dst_ref=back.at[device],
            send_sem=back_send_sem.at[device],
            recv_sem=back_recv_sem.at[device],
            device_id=to(device),
            device_id_type=pl.DeviceIdType.MESH,
        )

    for array in (energy_ext, tough_ext, prior_ext):
        array[:pad, :] = jnp.zeros((pad, LANES), F32)
        array[pad + cells :, :] = jnp.zeros((pad, LANES), F32)

    barrier = pltpu.get_barrier_semaphore()

    def greet(i):
        pl.semaphore_signal(
            barrier, inc=1, device_id=to(lax.rem(me + 1 + i, n)), device_id_type=pl.DeviceIdType.MESH
        )

    loop(n - 1, greet, unrolled)

    blocks = active_ref.shape[1]
    row, block = iota((cells, blocks), 0), iota((cells, blocks), 1)
    row_block = row // (4 * size_y) * BY + row % size_y // 4
    by_row = jnp.where(block // BZ == row_block, active_ref[...].astype(F32), 0.0).astype(BF16)
    by_lane = jnp.where(
        iota((LANES, blocks), 1) % BZ == iota((LANES, blocks), 0) // 4, 1.0, 0.0
    ).astype(BF16)
    live = dot_nt(by_row, by_lane)
    tough_ext[pad : pad + cells, :] = live * tough_ref[...]
    prior_ext[pad : pad + cells, :] = prior_ref[...]

    owner = owner_ref[...]
    owner_hot = jnp.where(iota((n, count), 0) == owner, 1.0, 0.0)
    chunks = count // LANES
    stacked = jnp.concatenate(
        [owner_hot[:, c * LANES : (c + 1) * LANES] for c in range(chunks)], axis=0
    ).astype(BF16)
    ahead = jnp.where(
        (iota((LANES, 2 * LANES), 0) < iota((LANES, 2 * LANES), 1))
        | (iota((LANES, 2 * LANES), 1) >= LANES),
        1.0,
        0.0,
    ).astype(BF16)
    counted = dot_nn(stacked, ahead)
    running = jnp.zeros((n, LANES), F32)
    places = []
    for c in range(chunks):
        part = counted[c * n : (c + 1) * n]
        hot = owner_hot[:, c * LANES : (c + 1) * LANES]
        places.append(jnp.sum(hot * (part[:, :LANES] + running), axis=0, keepdims=True))
        running = running + part[:, LANES:]
    place = jnp.concatenate(places, axis=1).astype(jnp.int32)
    place_hot = jnp.where(iota((LANES, count), 0) == place, 1.0, 0.0).astype(BF16)

    at_block, at_base = block_ref[...], base_ref[...]
    xy = (4 * (at_block // (BY * BZ)) + at_base // 9) * size_y
    xy = xy + 4 * (at_block // BZ % BY) + at_base // 3 % 3
    z = 4 * (at_block % BZ) + at_base % 3
    line = iota((8, count), 0)
    rest = jnp.where(
        line == 0,
        energy_ref[...],
        jnp.where(line == 1, xy.astype(F32), jnp.where(line == 2, z.astype(F32), 0.0)),
    )
    payload = jnp.concatenate(pieces(jnp.concatenate([weights_ref[...], rest], axis=0)), axis=0)
    group = min(n, 16)
    for first in range(0, n, group):
        chosen = []
        for device in range(first, first + group):
            mask = jnp.where(
                jnp.broadcast_to(owner, (3 * ROWS, count)) == device, 1.0, 0.0
            ).astype(BF16)
            chosen.append(payload * mask)
        bucket = dot_nt(jnp.concatenate(chosen, axis=0), place_hot)
        for i in range(group):
            part = bucket[3 * ROWS * i : 3 * ROWS * (i + 1)]
            send[first + i] = part[:ROWS] + part[ROWS : 2 * ROWS] + part[2 * ROWS :]

    pl.semaphore_wait(barrier, n - 1)

    loop(n - 1, lambda i: bucket_copy(lax.rem(me + 1 + i, n)).start(), unrolled)

    low, high = me > 0, me < n - 1
    end = pad + cells

    def upward(array, which, depth):
        return side_copy(
            which, array.at[pl.ds(end - depth, depth)], array.at[pl.ds(pad - depth, depth)], me + 1
        )

    def downward(array, which, depth):
        return side_copy(which, array.at[pl.ds(pad, depth)], array.at[pl.ds(end, depth)], me - 1)

    @pl.when(high)
    def _():
        upward(prior_ext, 0, pad).start()
        upward(tough_ext, 1, inner).start()

    @pl.when(low)
    def _():
        downward(prior_ext, 2, pad).start()
        downward(tough_ext, 3, inner).start()

    arrived[me] = send[me]
    total[...] = jnp.zeros_like(total)
    loop(n - 1, lambda i: bucket_arrival(lax.rem(me + n - 1 - i, n)).wait_recv(), unrolled)

    cell = iota((cells, LANES), 0)
    along = iota((LANES, LANES), 0)

    def gather_energy(pair):
        lefts, rights = [[], [], []], []
        for source in (2 * pair, 2 * pair + 1):
            rows = arrived[source]
            away = cell - rows[9:10].astype(jnp.int32)
            spread = []
            for k in range(2):
                spread.append(
                    jnp.where(
                        away == 0,
                        rows[k : k + 1],
                        jnp.where(
                            away == 1,
                            rows[k + 2 : k + 3],
                            jnp.where(
                                away == size_y,
                                rows[k + 4 : k + 5],
                                jnp.where(away == size_y + 1, rows[k + 6 : k + 7], 0.0),
                            ),
                        ),
                    )
                )
            spread = jnp.concatenate(spread, axis=0)
            mixed[source] = spread
            for held, piece in zip(lefts, pieces(spread * rows[8:9])):
                held.append(piece)
            hot = jnp.where(along == rows[10:11].astype(jnp.int32), 1.0, 0.0).astype(BF16)
            zhot[source] = hot
            rights.append(hot)
        left = jnp.concatenate(lefts[0] + lefts[1] + lefts[2], axis=1)
        total[...] += dot_nt(left, jnp.concatenate(rights * 3, axis=1))

    loop(n // 2, gather_energy, unrolled)
    energy_ext[pad:end, :] = total[:cells, :] + pltpu.roll(total[cells:, :], 1, 1)

    @pl.when(high)
    def _():
        upward(energy_ext, 4, inner).start()

    @pl.when(low)
    def _():
        downward(energy_ext, 5, inner).start()

    @pl.when(low)
    def _():
        upward(prior_ext, 0, pad).wait_recv()
        upward(tough_ext, 1, inner).wait_recv()
        upward(energy_ext, 4, inner).wait_recv()

    @pl.when(high)
    def _():
        downward(prior_ext, 2, pad).wait_recv()
        downward(tough_ext, 3, inner).wait_recv()
        downward(energy_ext, 5, inner).wait_recv()

    tough = tough_ext[...]
    twice = 2.0 * energy_ext[...]
    alive = tough > 0.0
    under = 1.0 / jnp.where(
        alive, twice + (1.0 / length_scale + 6.0 * length_scale) * tough, 1.0
    )
    couple = length_scale * tough * under
    source = jnp.where(alive, twice * under, 0.0)
    damage = prior_ext[...]
    rows = cells + 2 * pad
    row, lane = iota((rows, LANES), 0) % size_y, iota((rows, LANES), 1)
    blank = jnp.zeros((size_y, LANES), F32)
    for sweep in range(SWEEPS):
        beside = jnp.concatenate([damage[size_y:], blank], axis=0)
        beside = beside + jnp.concatenate([blank, damage[:-size_y]], axis=0)
        beside = beside + jnp.where(row == size_y - 1, 0.0, pltpu.roll(damage, rows - 1, 0))
        beside = beside + jnp.where(row == 0, 0.0, pltpu.roll(damage, 1, 0))
        beside = beside + jnp.where(lane == LANES - 1, 0.0, pltpu.roll(damage, LANES - 1, 1))
        beside = beside + jnp.where(lane == 0, 0.0, pltpu.roll(damage, 1, 1))
        damage = source + couple * beside
    damage = damage[pad:end]
    damage_ref[...] = damage

    both = jnp.concatenate([damage, pltpu.roll(damage, LANES - 1, 1)], axis=0)
    both = jnp.concatenate(pieces(both), axis=1)

    def sample(pair):
        hot = jnp.concatenate([zhot[2 * pair], zhot[2 * pair + 1]], axis=1)
        found = dot_nn(both, jnp.concatenate([hot] * 3, axis=0))
        for i in range(2):
            part = found[:, i * LANES : (i + 1) * LANES] * mixed[2 * pair + i]
            back_send[2 * pair + i] = jnp.sum(part, axis=0, keepdims=True)

    loop(n // 2, sample, unrolled)
    loop(n - 1, lambda i: back_copy(lax.rem(me + 1 + i, n)).start(), unrolled)
    back[me] = back_send[me]
    loop(n - 1, lambda i: back_arrival(lax.rem(me + n - 1 - i, n)).wait_recv(), unrolled)

    returned = jnp.concatenate([back[i] for i in range(n)], axis=0)
    found = dot_nn(jnp.concatenate(pieces(returned), axis=0), place_hot)
    found = found[:n] + found[n : 2 * n] + found[2 * n :]
    particle_damage = jnp.sum(found * owner_hot, axis=0, keepdims=True)
    factor = (1.0 - particle_damage) ** 2 + stiff_floor
    out_ref[...] = factor * stress_ref[...]

    def finish(i):
        device = lax.rem(me + 1 + i, n)
        bucket_copy(device).wait_send()
        back_copy(device).wait_send()

    loop(n - 1, finish, unrolled)

    @pl.when(high)
    def _():
        upward(prior_ext, 0, pad).wait_send()
        upward(tough_ext, 1, inner).wait_send()
        upward(energy_ext, 4, inner).wait_send()

    @pl.when(low)
    def _():
        downward(prior_ext, 2, pad).wait_send()
        downward(tough_ext, 3, inner).wait_send()
        downward(energy_ext, 5, inner).wait_send()


def body(
    crack_energy,
    weights,
    elastic_stress,
    owner_rank,
    local_block,
    base_cell,
    prior_damage,
    toughness,
    active_block,
):
    n = lax.axis_size("blk")
    count = crack_energy.shape[0]
    size_x, size_y, size_z = prior_damage.shape
    assert size_z == LANES and 2 * count // n <= LANES and size_x >= SWEEPS
    cells = size_x * size_y
    rows = cells + 2 * SWEEPS * size_y
    vmem = pl.BlockSpec(memory_space=pltpu.VMEM)
    damage, stress = pl.pallas_call(
        functools.partial(kernel, n, size_x, size_y),
        out_shape=(
            jax.ShapeDtypeStruct((cells, LANES), F32),
            jax.ShapeDtypeStruct(elastic_stress.shape, F32),
        ),
        in_specs=[vmem] * 9,
        out_specs=(vmem, vmem),
        scratch_shapes=[
            pltpu.VMEM((n, ROWS, LANES), F32),
            pltpu.VMEM((n, ROWS, LANES), F32),
            pltpu.VMEM((n, 2 * cells, LANES), F32),
            pltpu.VMEM((n, LANES, LANES), BF16),
            pltpu.VMEM((2 * cells, LANES), F32),
            pltpu.VMEM((rows, LANES), F32),
            pltpu.VMEM((rows, LANES), F32),
            pltpu.VMEM((rows, LANES), F32),
            pltpu.VMEM((n, 1, LANES), F32),
            pltpu.VMEM((n, 1, LANES), F32),
            pltpu.SemaphoreType.DMA((n,)),
            pltpu.SemaphoreType.DMA((n,)),
            pltpu.SemaphoreType.DMA((n,)),
            pltpu.SemaphoreType.DMA((n,)),
            pltpu.SemaphoreType.DMA((6,)),
            pltpu.SemaphoreType.DMA((6,)),
        ],
        compiler_params=pltpu.CompilerParams(
            collective_id=0,
            has_side_effects=True,
            vmem_limit_bytes=(24 if n <= 16 else 56) * 1024 * 1024,
        ),
    )(
        crack_energy.reshape(1, count),
        weights,
        elastic_stress,
        owner_rank.reshape(1, count),
        local_block.reshape(1, count),
        base_cell.reshape(1, count),
        prior_damage.reshape(cells, LANES),
        toughness.reshape(cells, LANES),
        active_block.reshape(1, active_block.shape[0]),
    )
    return (damage.reshape(prior_damage.shape), stress)


def solution(mesh):
    return jax.shard_map(
        body,
        mesh=mesh,
        in_specs=(
            P(("groups", "blk")),
            P(None, ("groups", "blk")),
            P(None, ("groups", "blk")),
            P(("groups", "blk"), None),
            P(("groups", "blk")),
            P(("groups", "blk")),
            P(("groups", "blk"), None, None),
            P(("groups", "blk"), None, None),
            P(("groups", "blk")),
        ),
        out_specs=(P(("groups", "blk"), None, None), P(None, ("groups", "blk"))),
        check_vma=False,
    )
```

time: 308 us -> 28.6 us (0.09)
  local copies, waits for them, and re-layouts: 118 us -> 5.82 us
  other arithmetic: 110 us -> 0 us
  starting transfers between devices: 51.3 us -> 0 us
  Pallas kernels: 0 us -> 21.7 us
  blocking collectives: 16.9 us -> 0 us
  waiting for transfers between devices: 9.97 us -> 0 us
    gather x4 -> x0, local copies, waits for them, and re-layouts: 102 us -> none  [the longest x1 90.5 us: body(): sampled = jnp.sum(arrived[1:] * damage.ravel()[local_index], axis=0)]
    scatter-add x2 -> x0, other arithmetic: 93.6 us -> none  [the longest x1 86 us: body(): jnp.zeros((cells_dev,), jnp.float32).at[local_index.ravel()]]
    ppermute x8 -> x0, starting transfers between devices: 37 us -> none  [the longest x4 31.8 us: extended_2(): lax.ppermute(tail, axis, [(i, (i + 1) % count) for i in range(ends)])]
    pallas_call x0 -> x1, Pallas kernels: none -> 21.7 us  [body(): pl.pallas_call(functools.partial(kernel, n, size_x, size_y), out_shape=(j...]
    all_to_all x1 -> x0, blocking collectives: 16.9 us -> none  [body(): lax.all_to_all(sampled, 'blk', split_axis=0, concat_axis=0, tiled=True)]
    all_to_all x2 -> x0, starting transfers between devices: 14.4 us -> none  [the longest x1 7.36 us: body(): lax.all_to_all(codes, 'blk', split_axis=1, concat_axis=1, tiled=True)]
    scatter x3 -> x0, local copies, waits for them, and re-layouts: 12.5 us -> none  [the longest x1 4.88 us: body(): jnp.full((devices * capacity,), -1, jnp.int32).at[buffer_index]]
    all_to_all x2 -> x0, waiting for transfers between devices: 7.69 us -> none  [the longest x1 7.68 us: body(): lax.all_to_all(packed, 'blk', split_axis=1, concat_axis=1, tiled=True)]
  transfers between devices with their start and end apart: 10 -> 0, of which waited for: 4 -> 0; matrix products, arithmetic and copies ran while one was open for 2% -> 0% of each run, Pallas kernels for 0% -> 0%
where the time goes in v1:
time: 28.6 us; the launch traced here: 28.2 us
  Pallas kernels  21.7 us (76%)
  local copies, waits for them, and re-layouts  5.82 us (20%)
  between operations  0.68 us (2%)
    pallas_call x1, Pallas kernels, body(): pl.pallas_call(functools.partial(kernel, n, size_x, size_y), out_shape=(j...  21.7 us
    unnamed x20, local copies, waits for them, and re-layouts  5.82 us

profile of v1, /device:TPU:0, one launch (start us, length us, event | category | flops | bytes accessed | tf_op | source)
XLA Modules:
  0.0 28.2 jit_solution(4775580144011252361)
XLA Ops:
  0.6 0.0 copy-start.6
  0.6 0.0 copy-start.5
  0.7 0.0 copy-start.4
  0.7 0.0 copy-start.8
  0.7 0.6 %copy-done.6 = s32[1024]{0:T(1024)S(1)} copy-done((s32[1024]{0:T(1024)S(1)}, s32[1024]{0:T(1024)}, u32[]{:S(2)}) %copy-start.6) | copy-done | bytes 4120
  1.3 0.0 copy-done.5
  1.3 0.0 copy-done.4
  1.4 0.0 copy-done.8
  1.4 0.0 copy-start
  1.4 0.8 %copy-done = f32[8,16,128]{2,1,0:T(8,128)S(1)} copy-done((f32[8,16,128]{2,1,0:T(8,128)S(1)}, f32[8,16,128]{2,1,0:T(8,128)}, u32[]{:S(2)}) %copy-start) | copy-done | bytes 65560
  2.2 0.0 copy-start.1
  2.2 0.8 %copy-done.1 = f32[8,16,128]{2,1,0:T(8,128)S(1)} copy-done((f32[8,16,128]{2,1,0:T(8,128)S(1)}, f32[8,16,128]{2,1,0:T(8,128)}, u32[]{:S(2)}) %copy-start.1) | copy-done | bytes 65560
  3.0 0.0 copy-start.2
  3.0 0.8 %copy-done.2 = f32[8,1024]{1,0:T(8,128)S(1)} copy-done((f32[8,1024]{1,0:T(8,128)S(1)}, f32[8,1024]{1,0:T(8,128)}, u32[]{:S(2)}) %copy-start.2) | copy-done | bytes 32792
  3.8 0.0 copy-start.3
  3.8 0.8 %copy-done.3 = f32[6,1024]{1,0:T(8,128)S(1)} copy-done((f32[6,1024]{1,0:T(8,128)S(1)}, f32[6,1024]{1,0:T(8,128)}, u32[]{:S(2)}) %copy-start.3) | copy-done | bytes 24600
  4.6 0.0 copy-start.7
  4.6 0.7 %copy-done.7 = s32[1024]{0:T(1024)S(1)} copy-done((s32[1024]{0:T(1024)S(1)}, s32[1024]{0:T(1024)}, u32[]{:S(2)}) %copy-start.7) | copy-done | bytes 4120
  5.2 21.7 %shard_map.104 = (f32[128,128]{1,0:T(8,128)S(1)}, f32[6,1024]{1,0:T(8,128)S(1)}) custom-call(f32[1,1024]{1,0:T(1,128)S(1)} %bitcast.11, f32[8,1024]{1,0:T(8,128)S(1)} %copy-done.2, f32[6,1024]{1,0:T(8,128)S(1)} %copy-done.3, s32[1,1024]{1,0:T(1,128)S(1)} %bitcast.12, s32[1,1024]{1,0:T(1,128)S(1)} %bitcast.13, s32[1,1024]{1,0:T(1,128)S(1)} %bitcast.14, ...), custom_call_target="tpu_custom_call" | custom-call | tf_op jit(solution)/shard_map/pallas_call | solution.py:384
  26.9 0.6 %copy.13 = f32[8,16,128]{2,1,0:T(8,128)} copy(f32[8,16,128]{2,1,0:T(8,128)S(1)} %bitcast.10) | data formatting | bytes 131072
  27.6 0.6 %copy.14 = f32[6,1024]{1,0:T(8,128)} copy(f32[6,1024]{1,0:T(8,128)S(1)} %get-tuple-element.9) | data formatting | bytes 49152
Async XLA Ops:
  0.6 0.7 %copy-start.6 = (s32[1024]{0:T(1024)S(1)}, s32[1024]{0:T(1024)}, u32[]{:S(2)}) copy-start(s32[1024]{0:T(1024)} %param.13) | copy-start | bytes 12292
  0.6 0.7 %copy-start.5 = (s32[1024,1]{0,1:T(1,128)S(1)}, s32[1024,1]{0,1:T(1,128)}, u32[]{:S(2)}) copy-start(s32[1024,1]{0,1:T(1,128)} %param.12) | copy-start | bytes 12292
  0.7 0.7 %copy-start.4 = (f32[1024]{0:T(1024)S(1)}, f32[1024]{0:T(1024)}, u32[]{:S(2)}) copy-start(f32[1024]{0:T(1024)} %param.9) | copy-start | bytes 12292
  0.7 0.7 %copy-start.8 = (s32[256]{0:T(256)S(1)}, s32[256]{0:T(256)}, u32[]{:S(2)}) copy-start(s32[256]{0:T(256)} %param.17) | copy-start | bytes 3076
  1.4 0.8 %copy-start = (f32[8,16,128]{2,1,0:T(8,128)S(1)}, f32[8,16,128]{2,1,0:T(8,128)}, u32[]{:S(2)}) copy-start(f32[8,16,128]{2,1,0:T(8,128)} %param.15) | copy-start | bytes 196612
  2.2 0.8 %copy-start.1 = (f32[8,16,128]{2,1,0:T(8,128)S(1)}, f32[8,16,128]{2,1,0:T(8,128)}, u32[]{:S(2)}) copy-start(f32[8,16,128]{2,1,0:T(8,128)} %param.16) | copy-start | bytes 196612
  3.0 0.8 %copy-start.2 = (f32[8,1024]{1,0:T(8,128)S(1)}, f32[8,1024]{1,0:T(8,128)}, u32[]{:S(2)}) copy-start(f32[8,1024]{1,0:T(8,128)} %weights_ref.1) | copy-start | bytes 98308
  3.8 0.8 %copy-start.3 = (f32[6,1024]{1,0:T(8,128)S(1)}, f32[6,1024]{1,0:T(8,128)}, u32[]{:S(2)}) copy-start(f32[6,1024]{1,0:T(8,128)} %stress_ref.1) | copy-start | bytes 73732
  4.6 0.7 %copy-start.7 = (s32[1024]{0:T(1024)S(1)}, s32[1024]{0:T(1024)}, u32[]{:S(2)}) copy-start(s32[1024]{0:T(1024)} %param.14) | copy-start | bytes 12292

commit v2 on v1

--- a/solution.py
+++ b/solution.py
@@ -12,6 +12,8 @@
 SWEEPS = 4
 LANES = 128
 ROWS = 16
+USED = 10
+GROUP = 4
 
 length_scale = 2.0
 stiff_floor = 0.001
@@ -52,17 +54,25 @@
     n,
     size_x,
     size_y,
+    energy_in,
+    weights_in,
+    stress_in,
+    owner_in,
+    block_in,
+    base_in,
+    prior_in,
+    tough_in,
+    active_in,
+    damage_ref,
+    out_ref,
     energy_ref,
     weights_ref,
     stress_ref,
     owner_ref,
     block_ref,
     base_ref,
-    prior_ref,
     tough_ref,
     active_ref,
-    damage_ref,
-    out_ref,
     send,
     arrived,
     mixed,
@@ -79,11 +89,30 @@
     back_recv_sem,
     side_send_sem,
     side_recv_sem,
+    load_sem,
 ):
     me = lax.axis_index("blk")
     cells = size_x * size_y
     count = owner_ref.shape[1]
     pad = SWEEPS * size_y
+    loads = [
+        pltpu.make_async_copy(source, target, load_sem.at[i])
+        for i, (source, target) in enumerate(
+            (
+                (owner_in, owner_ref),
+                (block_in, block_ref),
+                (base_in, base_ref),
+                (energy_in, energy_ref),
+                (weights_in, weights_ref),
+                (active_in, active_ref),
+                (tough_in, tough_ref),
+                (prior_in, prior_ext.at[pl.ds(pad, cells)]),
+                (stress_in, stress_ref),
+            )
+        )
+    ]
+    for load in loads:
+        load.start()
     inner = (SWEEPS - 1) * size_y
     unrolled = n <= 16
 
@@ -100,45 +129,33 @@
             device_id_type=pl.DeviceIdType.MESH,
         )
 
-    def bucket_copy(device):
+    def partner(i):
+        device, bit = 0, 1
+        while bit < n:
+            mine = lax.rem(lax.div(me, jnp.int32(bit)), jnp.int32(2))
+            if isinstance(i, int):
+                mine = 1 - mine if i // bit % 2 else mine
+            else:
+                mine = lax.rem(mine + lax.div(i, jnp.int32(bit)), jnp.int32(2))
+            device, bit = device + mine * bit, 2 * bit
+        return device
+
+    def swap(i, source, target, sends, receives):
         return pltpu.make_async_remote_copy(
-            src_ref=send.at[device],
-            dst_ref=arrived.at[me],
-            send_sem=send_sem.at[device],
-            recv_sem=recv_sem.at[me],
-            device_id=to(device),
+            src_ref=source,
+            dst_ref=target,
+            send_sem=sends.at[i],
+            recv_sem=receives.at[i],
+            device_id=to(partner(i)),
             device_id_type=pl.DeviceIdType.MESH,
         )
 
-    def bucket_arrival(device):
-        return pltpu.make_async_remote_copy(
-            src_ref=send.at[device],
-            dst_ref=arrived.at[device],
-            send_sem=send_sem.at[device],
-            recv_sem=recv_sem.at[device],
-            device_id=to(device),
-            device_id_type=pl.DeviceIdType.MESH,
-        )
-
-    def back_copy(device):
-        return pltpu.make_async_remote_copy(
-            src_ref=back_send.at[device],
-            dst_ref=back.at[me],
-            send_sem=back_send_sem.at[device],
-            recv_sem=back_recv_sem.at[me],
-            device_id=to(device),
-            device_id_type=pl.DeviceIdType.MESH,
-        )
-
-    def back_arrival(device):
-        return pltpu.make_async_remote_copy(
-            src_ref=back_send.at[device],
-            dst_ref=back.at[device],
-            send_sem=back_send_sem.at[device],
-            recv_sem=back_recv_sem.at[device],
-            device_id=to(device),
-            device_id_type=pl.DeviceIdType.MESH,
-        )
+    def bucket_copy(i):
+        used = pl.ds(0, USED)
+        return swap(i, send.at[i, used], arrived.at[i, used], send_sem, recv_sem)
+
+    def back_copy(i):
+        return swap(i, back_send.at[i], back.at[i], back_send_sem, back_recv_sem)
 
     for array in (energy_ext, tough_ext, prior_ext):
         array[:pad, :] = jnp.zeros((pad, LANES), F32)
@@ -148,23 +165,13 @@
 
     def greet(i):
         pl.semaphore_signal(
-            barrier, inc=1, device_id=to(lax.rem(me + 1 + i, n)), device_id_type=pl.DeviceIdType.MESH
+            barrier, inc=1, device_id=to(partner(i + 1)), device_id_type=pl.DeviceIdType.MESH
         )
 
     loop(n - 1, greet, unrolled)
 
-    blocks = active_ref.shape[1]
-    row, block = iota((cells, blocks), 0), iota((cells, blocks), 1)
-    row_block = row // (4 * size_y) * BY + row % size_y // 4
-    by_row = jnp.where(block // BZ == row_block, active_ref[...].astype(F32), 0.0).astype(BF16)
-    by_lane = jnp.where(
-        iota((LANES, blocks), 1) % BZ == iota((LANES, blocks), 0) // 4, 1.0, 0.0
-    ).astype(BF16)
-    live = dot_nt(by_row, by_lane)
-    tough_ext[pad : pad + cells, :] = live * tough_ref[...]
-    prior_ext[pad : pad + cells, :] = prior_ref[...]
-
-    owner = owner_ref[...]
+    loads[0].wait()
+    owner = jnp.bitwise_xor(owner_ref[...], me)
     owner_hot = jnp.where(iota((n, count), 0) == owner, 1.0, 0.0)
     chunks = count // LANES
     stacked = jnp.concatenate(
@@ -187,6 +194,8 @@
     place = jnp.concatenate(places, axis=1).astype(jnp.int32)
     place_hot = jnp.where(iota((LANES, count), 0) == place, 1.0, 0.0).astype(BF16)
 
+    for load in loads[1:5]:
+        load.wait()
     at_block, at_base = block_ref[...], base_ref[...]
     xy = (4 * (at_block // (BY * BZ)) + at_base // 9) * size_y
     xy = xy + 4 * (at_block // BZ % BY) + at_base // 3 % 3
@@ -195,25 +204,48 @@
     rest = jnp.where(
         line == 0,
         energy_ref[...],
-        jnp.where(line == 1, xy.astype(F32), jnp.where(line == 2, z.astype(F32), 0.0)),
+        jnp.where(line == 1, (xy * LANES + z).astype(F32), 0.0),
     )
-    payload = jnp.concatenate(pieces(jnp.concatenate([weights_ref[...], rest], axis=0)), axis=0)
-    group = min(n, 16)
-    for first in range(0, n, group):
+    payload = pieces(jnp.concatenate([weights_ref[...], rest], axis=0))
+    wide_owner = jnp.broadcast_to(owner, (ROWS, count))
+
+    def fill(group):
+        first = n - GROUP - GROUP * group
         chosen = []
-        for device in range(first, first + group):
-            mask = jnp.where(
-                jnp.broadcast_to(owner, (3 * ROWS, count)) == device, 1.0, 0.0
-            ).astype(BF16)
-            chosen.append(payload * mask)
+        for i in range(GROUP):
+            mask = jnp.where(wide_owner == first + i, 1.0, 0.0).astype(BF16)
+            chosen += [piece * mask for piece in payload]
         bucket = dot_nt(jnp.concatenate(chosen, axis=0), place_hot)
-        for i in range(group):
+        for i in range(GROUP):
             part = bucket[3 * ROWS * i : 3 * ROWS * (i + 1)]
             send[first + i] = part[:ROWS] + part[ROWS : 2 * ROWS] + part[2 * ROWS :]
-
+        return first
+
+    def fill_and_send(group):
+        first = fill(group)
+        for i in range(GROUP):
+            bucket_copy(first + i).start()
+
+    loop(1, fill, True)
     pl.semaphore_wait(barrier, n - 1)
-
-    loop(n - 1, lambda i: bucket_copy(lax.rem(me + 1 + i, n)).start(), unrolled)
+    for i in range(GROUP):
+        bucket_copy(n - GROUP + i).start()
+    loop(n // GROUP - 2, lambda group: fill_and_send(group + 1), unrolled)
+    fill(n // GROUP - 1)
+    for i in range(1, GROUP):
+        bucket_copy(i).start()
+
+    for load in loads[5:8]:
+        load.wait()
+    blocks = active_ref.shape[1]
+    row, block = iota((cells, blocks), 0), iota((cells, blocks), 1)
+    row_block = row // (4 * size_y) * BY + row % size_y // 4
+    by_row = jnp.where(block // BZ == row_block, active_ref[...].astype(F32), 0.0).astype(BF16)
+    by_lane = jnp.where(
+        iota((LANES, blocks), 1) % BZ == iota((LANES, blocks), 0) // 4, 1.0, 0.0
+    ).astype(BF16)
+    live = dot_nt(by_row, by_lane)
+    tough_ext[pad : pad + cells, :] = live * tough_ref[...]
 
     low, high = me > 0, me < n - 1
     end = pad + cells
@@ -236,18 +268,22 @@
         downward(prior_ext, 2, pad).start()
         downward(tough_ext, 3, inner).start()
 
-    arrived[me] = send[me]
+    arrived[0] = send[0]
     total[...] = jnp.zeros_like(total)
-    loop(n - 1, lambda i: bucket_arrival(lax.rem(me + n - 1 - i, n)).wait_recv(), unrolled)
 
     cell = iota((cells, LANES), 0)
     along = iota((LANES, LANES), 0)
 
-    def gather_energy(pair):
+    def gather_energy(group):
         lefts, rights = [[], [], []], []
-        for source in (2 * pair, 2 * pair + 1):
-            rows = arrived[source]
-            away = cell - rows[9:10].astype(jnp.int32)
+        for i in range(GROUP):
+            source = GROUP * group + i
+            if not (isinstance(source, int) and source == 0):
+                bucket_copy(source).wait_recv()
+        for i in range(GROUP):
+            source = GROUP * group + i
+            rows, code = arrived[source, :8], arrived[source, 9:10].astype(jnp.int32)
+            away = cell - code // LANES
             spread = []
             for k in range(2):
                 spread.append(
@@ -267,15 +303,16 @@
                 )
             spread = jnp.concatenate(spread, axis=0)
             mixed[source] = spread
-            for held, piece in zip(lefts, pieces(spread * rows[8:9])):
+            for held, piece in zip(lefts, pieces(spread * arrived[source, 8:9])):
                 held.append(piece)
-            hot = jnp.where(along == rows[10:11].astype(jnp.int32), 1.0, 0.0).astype(BF16)
+            hot = jnp.where(along == code % LANES, 1.0, 0.0).astype(BF16)
             zhot[source] = hot
             rights.append(hot)
         left = jnp.concatenate(lefts[0] + lefts[1] + lefts[2], axis=1)
         total[...] += dot_nt(left, jnp.concatenate(rights * 3, axis=1))
 
-    loop(n // 2, gather_energy, unrolled)
+    gather_energy(0)
+    loop(n // GROUP - 1, lambda group: gather_energy(group + 1), unrolled)
     energy_ext[pad:end, :] = total[:cells, :] + pltpu.roll(total[cells:, :], 1, 1)
 
     @pl.when(high)
@@ -324,29 +361,36 @@
     both = jnp.concatenate([damage, pltpu.roll(damage, LANES - 1, 1)], axis=0)
     both = jnp.concatenate(pieces(both), axis=1)
 
-    def sample(pair):
-        hot = jnp.concatenate([zhot[2 * pair], zhot[2 * pair + 1]], axis=1)
+    def sample(step):
+        first = n - 2 - 2 * step
+        hot = jnp.concatenate([zhot[first], zhot[first + 1]], axis=1)
         found = dot_nn(both, jnp.concatenate([hot] * 3, axis=0))
         for i in range(2):
-            part = found[:, i * LANES : (i + 1) * LANES] * mixed[2 * pair + i]
-            back_send[2 * pair + i] = jnp.sum(part, axis=0, keepdims=True)
-
-    loop(n // 2, sample, unrolled)
-    loop(n - 1, lambda i: back_copy(lax.rem(me + 1 + i, n)).start(), unrolled)
-    back[me] = back_send[me]
-    loop(n - 1, lambda i: back_arrival(lax.rem(me + n - 1 - i, n)).wait_recv(), unrolled)
+            part = found[:, i * LANES : (i + 1) * LANES] * mixed[first + i]
+            back_send[first + i] = jnp.sum(part, axis=0, keepdims=True)
+
+    def sample_and_send(step):
+        sample(step)
+        back_copy(n - 2 - 2 * step).start()
+        back_copy(n - 1 - 2 * step).start()
+
+    loop(n // 2 - 1, sample_and_send, unrolled)
+    sample(n // 2 - 1)
+    back_copy(1).start()
+    back[0] = back_send[0]
+    loop(n - 1, lambda i: back_copy(i + 1).wait_recv(), unrolled)
 
     returned = jnp.concatenate([back[i] for i in range(n)], axis=0)
     found = dot_nn(jnp.concatenate(pieces(returned), axis=0), place_hot)
     found = found[:n] + found[n : 2 * n] + found[2 * n :]
     particle_damage = jnp.sum(found * owner_hot, axis=0, keepdims=True)
     factor = (1.0 - particle_damage) ** 2 + stiff_floor
+    loads[8].wait()
     out_ref[...] = factor * stress_ref[...]
 
     def finish(i):
-        device = lax.rem(me + 1 + i, n)
-        bucket_copy(device).wait_send()
-        back_copy(device).wait_send()
+        bucket_copy(i + 1).wait_send()
+        back_copy(i + 1).wait_send()
 
     loop(n - 1, finish, unrolled)
 
@@ -377,6 +421,7 @@
     n = lax.axis_size("blk")
     count = crack_energy.shape[0]
     size_x, size_y, size_z = prior_damage.shape
+    assert n >= 2 * GROUP and n & (n - 1) == 0
     assert size_z == LANES and 2 * count // n <= LANES and size_x >= SWEEPS
     cells = size_x * size_y
     rows = cells + 2 * SWEEPS * size_y
@@ -387,9 +432,17 @@
             jax.ShapeDtypeStruct((cells, LANES), F32),
             jax.ShapeDtypeStruct(elastic_stress.shape, F32),
         ),
-        in_specs=[vmem] * 9,
+        in_specs=[pl.BlockSpec(memory_space=pltpu.HBM)] * 9,
         out_specs=(vmem, vmem),
         scratch_shapes=[
+            pltpu.VMEM((1, count), F32),
+            pltpu.VMEM(weights.shape, F32),
+            pltpu.VMEM(elastic_stress.shape, F32),
+            pltpu.VMEM((1, count), jnp.int32),
+            pltpu.VMEM((1, count), jnp.int32),
+            pltpu.VMEM((1, count), jnp.int32),
+            pltpu.VMEM((cells, LANES), F32),
+            pltpu.VMEM((1, active_block.shape[0]), jnp.int32),
             pltpu.VMEM((n, ROWS, LANES), F32),
             pltpu.VMEM((n, ROWS, LANES), F32),
             pltpu.VMEM((n, 2 * cells, LANES), F32),
@@ -406,11 +459,12 @@
             pltpu.SemaphoreType.DMA((n,)),
             pltpu.SemaphoreType.DMA((6,)),
             pltpu.SemaphoreType.DMA((6,)),
+            pltpu.SemaphoreType.DMA((9,)),
         ],
         compiler_params=pltpu.CompilerParams(
             collective_id=0,
             has_side_effects=True,
-            vmem_limit_bytes=(24 if n <= 16 else 56) * 1024 * 1024,
+            vmem_limit_bytes=60 * 1024 * 1024,
         ),
     )(
         crack_energy.reshape(1, count),

time: 28.6 us -> 24.2 us (0.85)
  local copies, waits for them, and re-layouts: 5.82 us -> 2.1 us
  Pallas kernels: 21.7 us -> 21.3 us
    unnamed x20 -> x4, local copies, waits for them, and re-layouts: 5.82 us -> 2.1 us
    pallas_call x1, Pallas kernels: 21.7 us -> 21.3 us  [body(): pl.pallas_call(functools.partial(kernel, n, size_x, size_y), out_shape=(j...]
where the time goes in v2:
time: 24.2 us; the launch traced here: 24 us
  Pallas kernels  21.3 us (88%)
  local copies, waits for them, and re-layouts  2.1 us (9%)
  between operations  0.65 us (3%)
    pallas_call x1, Pallas kernels, body(): pl.pallas_call(functools.partial(kernel, n, size_x, size_y), out_shape=(j...  21.3 us
    unnamed x4, local copies, waits for them, and re-layouts  2.1 us

profile of v2, /device:TPU:0, one launch (start us, length us, event | category | flops | bytes accessed | tf_op | source)
XLA Modules:
  0.0 24.0 jit_solution(7097575412009617018)
XLA Ops:
  0.6 21.3 %shard_map.104 = (f32[128,128]{1,0:T(8,128)}, f32[6,1024]{1,0:T(8,128)}) custom-call(f32[1,1024]{1,0:T(1,128)} %bitcast.11, f32[8,1024]{1,0:T(8,128)} %weights_in.1, f32[6,1024]{1,0:T(8,128)} %stress_in.1, s32[1,1024]{1,0:T(1,128)} %bitcast.12, s32[1,1024]{1,0:T(1,128)} %bitcast.13, s32[1,1024]{1,0:T(1,128)} %bitcast.14, f32[128,128]{1,0:T(8,128)} %bitcast.8, ...), custom_call_target="tpu_custom_call" | custom-call | tf_op jit(solution)/shard_map/pallas_call | solution.py:429
  21.9 0.0 copy-start
  21.9 1.5 %copy.13 = f32[8,16,128]{2,1,0:T(8,128)} copy(f32[8,16,128]{2,1,0:T(8,128)} %bitcast.10) | data formatting | bytes 131072
  23.4 0.0 copy-done
  23.4 0.6 %copy.14 = f32[6,1024]{1,0:T(8,128)} copy(f32[6,1024]{1,0:T(8,128)S(1)} %copy-done) | data formatting | bytes 49152
Async XLA Ops:
  21.9 1.5 %copy-start = (f32[6,1024]{1,0:T(8,128)S(1)}, f32[6,1024]{1,0:T(8,128)}, u32[]{:S(2)}) copy-start(f32[6,1024]{1,0:T(8,128)} %get-tuple-element.9) | copy-start | bytes 73732

commit v3 on v2

--- a/solution.py
+++ b/solution.py
@@ -429,8 +429,8 @@
     damage, stress = pl.pallas_call(
         functools.partial(kernel, n, size_x, size_y),
         out_shape=(
-            jax.ShapeDtypeStruct((cells, LANES), F32),
-            jax.ShapeDtypeStruct(elastic_stress.shape, F32),
+            pltpu.VMEM((cells, LANES), F32),
+            pltpu.VMEM(elastic_stress.shape, F32),
         ),
         in_specs=[pl.BlockSpec(memory_space=pltpu.HBM)] * 9,
         out_specs=(vmem, vmem),

time: 24.2 us -> 22.7 us (0.938)
  local copies, waits for them, and re-layouts: 2.1 us -> 1.25 us
  Pallas kernels: 21.3 us -> 20.6 us
    unnamed x4 -> x2, local copies, waits for them, and re-layouts: 2.1 us -> 1.25 us
    pallas_call x1, Pallas kernels: 21.3 us -> 20.6 us  [body(): pl.pallas_call(functools.partial(kernel, n, size_x, size_y), out_shape=(p...]
where the time goes in v3:
time: 22.7 us; the launch traced here: 22.5 us
  Pallas kernels  20.6 us (91%)
  local copies, waits for them, and re-layouts  1.25 us (6%)
  between operations  0.64 us (3%)
    pallas_call x1, Pallas kernels, body(): pl.pallas_call(functools.partial(kernel, n, size_x, size_y), out_shape=(p...  20.6 us
    unnamed x2, local copies, waits for them, and re-layouts  1.25 us

profile of v3, /device:TPU:0, one launch (start us, length us, event | category | flops | bytes accessed | tf_op | source)
XLA Modules:
  0.0 22.5 jit_solution(17836331795502584181)
XLA Ops:
  0.6 20.6 %shard_map.104 = (f32[128,128]{1,0:T(8,128)S(1)}, f32[6,1024]{1,0:T(8,128)S(1)}) custom-call(f32[1,1024]{1,0:T(1,128)} %bitcast.11, f32[8,1024]{1,0:T(8,128)} %weights_in.1, f32[6,1024]{1,0:T(8,128)} %stress_in.1, s32[1,1024]{1,0:T(1,128)} %bitcast.12, s32[1,1024]{1,0:T(1,128)} %bitcast.13, s32[1,1024]{1,0:T(1,128)} %bitcast.14, f32[128,128]{1,0:T(8,128)} %bitcast.9, ...), custom_call_target="tpu_custom_call" | custom-call | tf_op jit(solution)/shard_map/pallas_call | solution.py:429
  21.3 0.6 %copy.13 = f32[8,16,128]{2,1,0:T(8,128)} copy(f32[8,16,128]{2,1,0:T(8,128)S(1)} %bitcast.8) | data formatting | bytes 131072
  21.9 0.6 %copy.14 = f32[6,1024]{1,0:T(8,128)} copy(f32[6,1024]{1,0:T(8,128)S(1)} %get-tuple-element.7) | data formatting | bytes 49152

commit v4 on v3

--- a/solution.py
+++ b/solution.py
@@ -47,7 +47,10 @@
         for i in range(count):
             step(i)
     else:
-        pl.loop(0, count)(step)
+
+        @pl.loop(0, count)
+        def _(i):
+            step(i)
 
 
 def kernel(
@@ -170,7 +173,8 @@
 
     loop(n - 1, greet, unrolled)
 
-    loads[0].wait()
+    for load in loads[:5]:
+        load.wait()
     owner = jnp.bitwise_xor(owner_ref[...], me)
     owner_hot = jnp.where(iota((n, count), 0) == owner, 1.0, 0.0)
     chunks = count // LANES
@@ -194,8 +198,6 @@
     place = jnp.concatenate(places, axis=1).astype(jnp.int32)
     place_hot = jnp.where(iota((LANES, count), 0) == place, 1.0, 0.0).astype(BF16)
 
-    for load in loads[1:5]:
-        load.wait()
     at_block, at_base = block_ref[...], base_ref[...]
     xy = (4 * (at_block // (BY * BZ)) + at_base // 9) * size_y
     xy = xy + 4 * (at_block // BZ % BY) + at_base // 3 % 3
@@ -226,14 +228,9 @@
         for i in range(GROUP):
             bucket_copy(first + i).start()
 
-    loop(1, fill, True)
+    loop(n // GROUP, fill, unrolled)
     pl.semaphore_wait(barrier, n - 1)
-    for i in range(GROUP):
-        bucket_copy(n - GROUP + i).start()
-    loop(n // GROUP - 2, lambda group: fill_and_send(group + 1), unrolled)
-    fill(n // GROUP - 1)
-    for i in range(1, GROUP):
-        bucket_copy(i).start()
+    loop(n - 1, lambda i: bucket_copy(i + 1).start(), unrolled)
 
     for load in loads[5:8]:
         load.wait()
@@ -257,16 +254,6 @@
 
     def downward(array, which, depth):
         return side_copy(which, array.at[pl.ds(pad, depth)], array.at[pl.ds(end, depth)], me - 1)
-
-    @pl.when(high)
-    def _():
-        upward(prior_ext, 0, pad).start()
-        upward(tough_ext, 1, inner).start()
-
-    @pl.when(low)
-    def _():
-        downward(prior_ext, 2, pad).start()
-        downward(tough_ext, 3, inner).start()
 
     arrived[0] = send[0]
     total[...] = jnp.zeros_like(total)
@@ -312,6 +299,16 @@
         total[...] += dot_nt(left, jnp.concatenate(rights * 3, axis=1))
 
     gather_energy(0)
+    @pl.when(high)
+    def _():
+        upward(prior_ext, 0, pad).start()
+        upward(tough_ext, 1, inner).start()
+
+    @pl.when(low)
+    def _():
+        downward(prior_ext, 2, pad).start()
+        downward(tough_ext, 3, inner).start()
+
     loop(n // GROUP - 1, lambda group: gather_energy(group + 1), unrolled)
     energy_ext[pad:end, :] = total[:cells, :] + pltpu.roll(total[cells:, :], 1, 1)
 
@@ -362,21 +359,23 @@
     both = jnp.concatenate(pieces(both), axis=1)
 
     def sample(step):
-        first = n - 2 - 2 * step
-        hot = jnp.concatenate([zhot[first], zhot[first + 1]], axis=1)
+        first = n - GROUP - GROUP * step
+        hot = jnp.concatenate([zhot[first + i] for i in range(GROUP)], axis=1)
         found = dot_nn(both, jnp.concatenate([hot] * 3, axis=0))
-        for i in range(2):
+        for i in range(GROUP):
             part = found[:, i * LANES : (i + 1) * LANES] * mixed[first + i]
             back_send[first + i] = jnp.sum(part, axis=0, keepdims=True)
+        return first
 
     def sample_and_send(step):
-        sample(step)
-        back_copy(n - 2 - 2 * step).start()
-        back_copy(n - 1 - 2 * step).start()
-
-    loop(n // 2 - 1, sample_and_send, unrolled)
-    sample(n // 2 - 1)
-    back_copy(1).start()
+        first = sample(step)
+        for i in range(GROUP):
+            back_copy(first + i).start()
+
+    loop(n // GROUP - 1, sample_and_send, unrolled)
+    sample(n // GROUP - 1)
+    for i in range(1, GROUP):
+        back_copy(i).start()
     back[0] = back_send[0]
     loop(n - 1, lambda i: back_copy(i + 1).wait_recv(), unrolled)
 

time: 22.7 us -> 21.5 us (0.947)
  Pallas kernels: 20.6 us -> 19.4 us
    pallas_call x1, Pallas kernels: 20.6 us -> 19.4 us  [body(): pl.pallas_call(functools.partial(kernel, n, size_x, size_y), out_shape=(p...]
where the time goes in v4:
time: 21.5 us; the launch traced here: 21.3 us
  Pallas kernels  19.4 us (90%)
  local copies, waits for them, and re-layouts  1.25 us (6%)
  between operations  0.64 us (3%)
    pallas_call x1, Pallas kernels, body(): pl.pallas_call(functools.partial(kernel, n, size_x, size_y), out_shape=(p...  19.4 us
    unnamed x2, local copies, waits for them, and re-layouts  1.25 us

profile of v4, /device:TPU:0, one launch (start us, length us, event | category | flops | bytes accessed | tf_op | source)
XLA Modules:
  0.0 21.3 jit_solution(11003809423621230889)
XLA Ops:
  0.6 19.4 %shard_map.104 = (f32[128,128]{1,0:T(8,128)S(1)}, f32[6,1024]{1,0:T(8,128)S(1)}) custom-call(f32[1,1024]{1,0:T(1,128)} %bitcast.11, f32[8,1024]{1,0:T(8,128)} %weights_in.1, f32[6,1024]{1,0:T(8,128)} %stress_in.1, s32[1,1024]{1,0:T(1,128)} %bitcast.12, s32[1,1024]{1,0:T(1,128)} %bitcast.13, s32[1,1024]{1,0:T(1,128)} %bitcast.14, f32[128,128]{1,0:T(8,128)} %bitcast.9, ...), custom_call_target="tpu_custom_call" | custom-call | tf_op jit(solution)/shard_map/pallas_call | solution.py:428
  20.1 0.6 %copy.13 = f32[8,16,128]{2,1,0:T(8,128)} copy(f32[8,16,128]{2,1,0:T(8,128)S(1)} %bitcast.8) | data formatting | bytes 131072
  20.7 0.6 %copy.14 = f32[6,1024]{1,0:T(8,128)} copy(f32[6,1024]{1,0:T(8,128)S(1)} %get-tuple-element.7) | data formatting | bytes 49152

commit v5 on v4

--- a/solution.py
+++ b/solution.py
@@ -377,6 +377,25 @@
     for i in range(1, GROUP):
         back_copy(i).start()
     back[0] = back_send[0]
+
+    def finish(i):
+        bucket_copy(i + 1).wait_send()
+        back_copy(i + 1).wait_send()
+
+    loop(n - 1, finish, unrolled)
+
+    @pl.when(high)
+    def _():
+        upward(prior_ext, 0, pad).wait_send()
+        upward(tough_ext, 1, inner).wait_send()
+        upward(energy_ext, 4, inner).wait_send()
+
+    @pl.when(low)
+    def _():
+        downward(prior_ext, 2, pad).wait_send()
+        downward(tough_ext, 3, inner).wait_send()
+        downward(energy_ext, 5, inner).wait_send()
+
     loop(n - 1, lambda i: back_copy(i + 1).wait_recv(), unrolled)
 
     returned = jnp.concatenate([back[i] for i in range(n)], axis=0)
@@ -386,24 +405,6 @@
     factor = (1.0 - particle_damage) ** 2 + stiff_floor
     loads[8].wait()
     out_ref[...] = factor * stress_ref[...]
-
-    def finish(i):
-        bucket_copy(i + 1).wait_send()
-        back_copy(i + 1).wait_send()
-
-    loop(n - 1, finish, unrolled)
-
-    @pl.when(high)
-    def _():
-        upward(prior_ext, 0, pad).wait_send()
-        upward(tough_ext, 1, inner).wait_send()
-        upward(energy_ext, 4, inner).wait_send()
-
-    @pl.when(low)
-    def _():
-        downward(prior_ext, 2, pad).wait_send()
-        downward(tough_ext, 3, inner).wait_send()
-        downward(energy_ext, 5, inner).wait_send()
 
 
 def body(

time: 21.5 us -> 21.5 us (level)
  no operation moved by 1% of the time
where the time goes in v5:
time: 21.5 us; the launch traced here: 21.3 us
  Pallas kernels  19.4 us (90%)
  local copies, waits for them, and re-layouts  1.25 us (6%)
  between operations  0.64 us (3%)
    pallas_call x1, Pallas kernels, body(): pl.pallas_call(functools.partial(kernel, n, size_x, size_y), out_shape=(p...  19.4 us
    unnamed x2, local copies, waits for them, and re-layouts  1.25 us

profile of v5, /device:TPU:0, one launch (start us, length us, event | category | flops | bytes accessed | tf_op | source)
XLA Modules:
  0.0 21.3 jit_solution(17885913773868949519)
XLA Ops:
  0.6 19.4 %shard_map.104 = (f32[128,128]{1,0:T(8,128)S(1)}, f32[6,1024]{1,0:T(8,128)S(1)}) custom-call(f32[1,1024]{1,0:T(1,128)} %bitcast.11, f32[8,1024]{1,0:T(8,128)} %weights_in.1, f32[6,1024]{1,0:T(8,128)} %stress_in.1, s32[1,1024]{1,0:T(1,128)} %bitcast.12, s32[1,1024]{1,0:T(1,128)} %bitcast.13, s32[1,1024]{1,0:T(1,128)} %bitcast.14, f32[128,128]{1,0:T(8,128)} %bitcast.9, ...), custom_call_target="tpu_custom_call" | custom-call | tf_op jit(solution)/shard_map/pallas_call | solution.py:429
  20.0 0.6 %copy.13 = f32[8,16,128]{2,1,0:T(8,128)} copy(f32[8,16,128]{2,1,0:T(8,128)S(1)} %bitcast.8) | data formatting | bytes 131072
  20.7 0.6 %copy.14 = f32[6,1024]{1,0:T(8,128)} copy(f32[6,1024]{1,0:T(8,128)S(1)} %get-tuple-element.7) | data formatting | bytes 49152
